TPU v7x, 512 devices: a whole 4x4x16 slice. The times are simulated.
512 devices in a mesh: dp: 32 (over z, core), tensor: 16 (over x, y).
Axes of the slice: x: 4, y: 4, z: 16, core: 2. Of those that a mesh axis runs over, the one named last changes fastest.
Arguments:
- activations: bfloat16 [65536, 4096], P(('dp', 'tensor')), may hold values from -6 to 6
- grad_query: bfloat16 [65536, 4096], P('dp', 'tensor'), may hold values from -6 to 6
- feedback: bfloat16 [131072, 4096], P('dp', 'tensor'), may hold values from -256 to 256
- start_factor: float32 [8, 4096], P(None, 'tensor'), may hold values from -6 to 6
Outputs:
- basis: float32 [128, 4096], P('tensor')
- coeffs: float32 [8, 4096], P(None, 'tensor')
All inputs are finite; a program needn't handle non-finite values.
Results may differ from a plain program's by a relative error of at most 0.0003.
Values may be sent and summed in bfloat16 or wider, within the bound.
A program may use at most 64 MiB of HBM per device.

v0:
```python
import jax
import jax.numpy as jnp
from jax import lax
from jax.sharding import PartitionSpec as P

EPSILON = 1e-06
HIGHEST = lax.Precision.HIGHEST


def orthonormal_rows(factor):
    finished = []
    for position in range(factor.shape[0]):
        vector = factor[position]
        for earlier in finished:
            vector = vector - jnp.sum(earlier * vector) * earlier
        vector = vector / jnp.sqrt(jnp.sum(vector * vector) + EPSILON)
        finished.append(vector)
    return jnp.stack(finished)


def body(activations, grad_query, feedback, start_factor):
    replicas = lax.axis_size("dp")
    residual = feedback.astype(jnp.float32)
    own_left = lax.dot_general(start_factor, residual, (((1,), (1,)), ((), ())), precision=HIGHEST)
    grad_weight = lax.dot_general(
        lax.all_gather(activations, "tensor", axis=0, tiled=True),
        grad_query,
        (((0,), (0,)), ((), ())),
        preferred_element_type=jnp.float32,
    )
    local_left = (
        lax.dot_general(start_factor, grad_weight, (((1,), (1,)), ((), ())), precision=HIGHEST)
        + own_left
    )
    summed_left = lax.psum(local_left, "dp")
    basis = orthonormal_rows(summed_left)
    own_right = jnp.dot(basis, residual, precision=HIGHEST)
    local_right = jnp.dot(basis, grad_weight, precision=HIGHEST) + own_right
    coeffs = lax.psum(local_right, "dp") / replicas
    return (basis, coeffs)


def solution(mesh):
    in_specs = (P(("dp", "tensor"), None), P("dp", "tensor"), P("dp", "tensor"), P(None, "tensor"))
    out_specs = (P("tensor", None), P(None, "tensor"))
    return jax.shard_map(body, mesh=mesh, in_specs=in_specs, out_specs=out_specs, check_vma=False)
```

profile of v0, /device:TPU:1, one launch (start us, length us, event | category | flops | bytes accessed | tf_op | source)
XLA Modules:
  0.0 482.3 jit_solution(11696932838765392247)
XLA Ops:
  7.2 0.0 all-gather.2.cloned.1.call-start
  7.2 0.7 all-gather.2.cloned.1.call-update
  7.9 0.0 all-reduce.2.cloned.1.call-start
  8.0 135.0 %all-gather.2.cloned.1.call-done = bf16[2048,4096]{1,0:T(8,128)(2,1)} async-done(((bf16[128,4096]{1,0:T(8,128)(2,1)}), bf16[2048,4096]{1,0:T(8,128)(2,1)}) %all-gather.2.cloned.1.call-update) | async-done | bytes 16777232 | tf_op jit(solution)/shard_map/all_gather | solution.py:26
  143.0 8.9 %fusion.1 = f32[4096,256]{1,0:T(8,128)S(1)} fusion(bf16[2048,4096]{1,0:T(8,128)(2,1)} %all-gather.2.cloned.1.call-done, bf16[2048,256]{1,0:T(8,128)(2,1)} %param.5), kind=kOutput, calls=%fused_computation.82 | convolution fusion | flops 4294967296 | bytes 22020096 | tf_op jit(solution)/shard_map/dot_general | solution.py:25
  151.9 1.9 copy-done.1
  153.8 3.6 convolution_bitcast_fusion
  157.4 2.4 convolution_add_fusion
  159.8 0.0 all-reduce.2.cloned.1.call-update
  159.8 195.8 %all-reduce.2.cloned.1.call-done = f32[8,4096]{1,0:T(8,128)} async-done(((f32[8,4096]{1,0:T(8,128)}), f32[8,4096]{1,0:T(8,128)}) %all-reduce.2.cloned.1.call-update) | async-done | bytes 131088 | tf_op jit(solution)/shard_map/psum | solution.py:35
  355.6 1.5 multiply_reduce_fusion.35
  357.9 1.6 fusion
  359.5 0.6 multiply_reduce_fusion.34
  360.1 1.4 multiply_reduce_fusion.7
  362.2 5.0 %multiply_reduce_fusion.6 = (f32[]{:T(128)}, f32[]{:T(128)}, f32[]{:T(128)}, f32[]{:T(128)}, f32[]{:T(128)}, /*index=5*/f32[]{:T(128)}, f32[4096]{0:T(1024)S(1)}) fusion(f32[4096]{0:T(1024)S(1)} %bitcast.27, f32[4096]{0:T(1024)S(1)} %bitcast.22, f32[]{:T(128)} %get-tuple-element.22, f32[4096]{0:T(1024)S(1)} %bitcast.30, f32[]{:T(128)} %get-tuple-element.23, ...), kind=kLoop, calls=%fused_computation.15 | loop fusion | flops 110586 | bytes 147512 | tf_op jit(solution)/shard_map/reduce_sum | solution.py:15
  367.2 1.8 multiply_reduce_fusion.30
  369.7 2.0 multiply_reduce_fusion.27
  371.7 6.2 %multiply_reduce_fusion.5 = (f32[]{:T(128)}, f32[]{:T(128)}, f32[]{:T(128)}, f32[]{:T(128)}, f32[]{:T(128)}, /*index=5*/f32[4096]{0:T(1024)S(1)}, f32[4096]{0:T(1024)S(1)}, f32[4096]{0:T(1024)S(1)}, f32[4096]{0:T(1024)S(1)}) fusion(f32[4096]{0:T(1024)S(1)} %get-tuple-element.53, f32[]{:T(128)S(6)} %sqrt.26, f32[4096]{0:T(1024)S(1)} %get-tuple-element.51, ...), kind=kLoop, calls=%fused_computation.13 | loop fusion | flops 118779 | bytes 196668 | tf_op jit(solution)/shard_map/reduce_sum | solution.py:15
  378.6 3.9 multiply_reduce_fusion.4
  382.5 2.6 multiply_reduce_fusion.21
  385.8 2.6 multiply_reduce_fusion.16
  388.4 4.5 multiply_reduce_fusion.3
  393.4 2.5 multiply_reduce_fusion.2
  396.0 2.5 multiply_reduce_fusion.8
  399.2 2.5 multiply_reduce_fusion.1
  401.7 1.3 multiply_reduce_fusion
  403.7 19.3 %subtract_divide_fusion = (f32[1,4096]{1,0:T(1,128)S(1)}, f32[1,4096]{1,0:T(1,128)S(1)}, f32[1,4096]{1,0:T(1,128)S(1)}, f32[1,4096]{1,0:T(1,128)S(1)}, f32[1,409...) fusion(f32[1,4096]{1,0:T(1,128)S(1)} %get-tuple-element.56, f32[]{:T(128)S(6)} %sqrt.31, ...), kind=kLoop, calls=%fused_computation.4 | loop fusion | flops 258048 | bytes 245900 | tf_op jit(solution)/shard_map/div | solution.py:16
  423.0 0.2 stack.2
  423.2 4.0 fusion.2
  427.2 0.9 convolution_add_fusion.1
  428.1 46.7 %psum.15 = f32[8,256]{1,0:T(8,128)S(1)} all-reduce(f32[8,256]{1,0:T(8,128)S(1)} %convolution_add_fusion.1), channel_id=1, replica_groups=mesh['dp'=32,'tensor'=16] {'dp'}, use_global_device_ids=true, to_apply=%region_37.0 | all-reduce | flops 2048 | bytes 16384 | tf_op jit(solution)/shard_map/psum | solution.py:39
  474.8 0.6 broadcast_multiply_fusion
  (7 shorter events, 0.0 us)
Async XLA Ops:
  7.2 150.2 %copy-start = (bf16[4096,256]{1,0:T(8,128)(2,1)S(1)}, bf16[4096,256]{1,0:T(8,128)(2,1)}, u32[]{:S(2)}) copy-start(bf16[4096,256]{1,0:T(8,128)(2,1)} %param.6) | copy-start | bytes 6291460
  7.2 135.8 %all-gather.2.cloned.1.call-start = ((), (), s32[]{:S(2)}) async-start(), calls=%async_computation | async-start | bytes 17825792 | tf_op jit(solution)/shard_map/all_gather | solution.py:26
  7.9 145.9 %copy-start.3 = (f32[8,256]{1,0:T(8,128)S(1)}, f32[8,256]{1,0:T(8,128)}, u32[]{:S(2)}) copy-start(f32[8,256]{1,0:T(8,128)} %param.7) | copy-start | bytes 24580
  7.9 347.7 %all-reduce.2.cloned.1.call-start = ((), (), s32[]{:S(2)}) async-start(), calls=%async_computation.1 | async-start | bytes 262144 | tf_op jit(solution)/shard_map/psum | solution.py:35
  151.9 1.9 copy-start.1
  423.2 52.2 %copy-start.2 = (f32[8,4096]{1,0:T(8,128)}, f32[8,4096]{1,0:T(8,128)S(1)}, u32[]{:S(2)}) copy-start(f32[8,4096]{1,0:T(8,128)S(1)} %stack.2) | copy-start | bytes 393220
Sparse Core Ops, SparseCore 0:
  11.0 131.8 all-gather.1
  160.0 195.6 all-reduce.1
where the time goes:
time: 485 us; the launch traced here: 482 us
  waiting for transfers between devices  331 us (68%)
  other arithmetic  62.6 us (13%)
  blocking collectives  46.7 us (10%)
  matrix products  19.8 us (4%)
  between operations  19.5 us (4%)
    psum x1, waiting for transfers between devices, body(): summed_left = lax.psum(local_left, 'dp')  196 us
    all_gather x1, waiting for transfers between devices, body(): lax.all_gather(activations, 'tensor', axis=0, tiled=True)  135 us
    psum x1, blocking collectives, body(): coeffs = lax.psum(local_right, 'dp') / replicas  46.7 us
    reduce_sum x10, other arithmetic, orthonormal_rows(): vector = vector - jnp.sum(earlier * vector) * earlier  31.2 us
    div x1, other arithmetic, orthonormal_rows(): vector = vector / jnp.sqrt(jnp.sum(vector * vector) + EPSILON)  19.3 us
    reduce_sum x5, other arithmetic, orthonormal_rows(): vector = vector / jnp.sqrt(jnp.sum(vector * vector) + EPSILON)  9.81 us
  transfers between devices with their start and end apart: 2, of which 2 were waited for; matrix products, arithmetic and copies ran while one was open for 0% of the time, Pallas kernels for 0%

commit v1 on v0

v1 whole, which is shorter than its diff:
```python
import functools

import jax
import jax.numpy as jnp
from jax import lax
from jax.experimental import pallas as pl
from jax.experimental.pallas import tpu as pltpu
from jax.sharding import PartitionSpec as P

EPSILON = 1e-06
MESH = pl.DeviceIdType.MESH
F32, BF16 = jnp.float32, jnp.bfloat16
RANK = 8
LANES = 128
NT = (((1,), (1,)), ((), ()))
NN = (((1,), (0,)), ((), ()))


def dot(a, b, dims):
    return lax.dot_general(a, b, dims, preferred_element_type=F32)


def pair(value):
    top = value.astype(BF16).astype(F32)
    return jnp.concatenate([top, value - top], axis=0).astype(BF16)


def unpair(value):
    return value[:RANK] + value[RANK:]


def wait_bytes(ref, sem):
    pltpu.make_async_copy(ref, ref, sem).wait()


def kernel(
    nx, ny, nz,
    s_ref, g_hbm, a_hbm, f_hbm,
    basis_ref, coeffs_ref,
    g_v, a_v, f_v, gh_v, fh_v,
    psend, precv,
    la, lb, ra, rb, sa, sb, r2a, r2b,
    lf, lfr, zs, zr, full,
    bp, ball_a, ball_b,
    qs, qr, cr, cfin,
    local, send, recv,
):
    tn = nx * ny
    half = a_v.shape[1]
    quarter = half // 2
    tok = g_v.shape[0]
    dp, t = lax.axis_index("dp"), lax.axis_index("tensor")
    z, c = dp // 2, lax.rem(dp, 2)
    o = 1 - c
    x, y = t // ny, lax.rem(t, ny)
    partner = (2 * z + o, t)

    def cols(index, size):
        return pl.ds(pl.multiple_of(index * size, size), size)

    def rows(index, size):
        return pl.ds(pl.multiple_of(index * size, size), size)

    def remote(src, dst, index, device):
        return pltpu.make_async_remote_copy(
            src_ref=src, dst_ref=dst, send_sem=send.at[index], recv_sem=recv.at[index],
            device_id=device, device_id_type=MESH,
        )

    def plane(k):
        other = lax.rem(t + k // 2, tn)
        return other, (2 * z + lax.rem(c + lax.rem(k, 2), 2), other)

    def along_z(k):
        other = lax.rem(z + k, nz)
        return other, (2 * other + c, t)

    def along_x(k):
        other = lax.rem(x + k, nx)
        return other, (dp, other * ny + y)

    def along_y(k):
        other = lax.rem(y + k, ny)
        return other, (dp, x * ny + other)

    loads = [
        pltpu.make_async_copy(g_hbm, g_v, local.at[0]),
        pltpu.make_async_copy(a_hbm.at[:, cols(c, half)], a_v.at[rows(c, LANES), :], local.at[1]),
        pltpu.make_async_copy(f_hbm, f_v, local.at[2]),
        pltpu.make_async_copy(g_hbm.at[:, cols(c, LANES)], gh_v.at[c], local.at[3]),
        pltpu.make_async_copy(f_hbm.at[:, cols(c, LANES)], fh_v.at[c], local.at[4]),
    ]
    for load in loads:
        load.start()

    barrier = pltpu.get_barrier_semaphore()

    @pl.loop(1, 2 * tn)
    def _(k):
        pl.semaphore_signal(barrier, inc=1, device_id=plane(k)[1], device_id_type=MESH)

    @pl.loop(1, nz)
    def _(k):
        pl.semaphore_signal(barrier, inc=1, device_id=along_z(k)[1], device_id_type=MESH)

    s2 = pair(s_ref[...])
    loads[0].wait()
    p2 = pair(unpair(dot(s2, g_v[...], NT)))
    for k in range(tn):
        psend[k] = p2[:, k * LANES:(k + 1) * LANES]

    pl.semaphore_wait(barrier, 2 * tn - 1 + nz - 1)

    share_a = remote(a_hbm.at[:, cols(o, half)], a_v.at[rows(c, LANES), :], 0, partner)
    share_a.start()

    precv[rows(c * tn + t, 16), :] = psend[t]

    @pl.loop(1, 2 * tn)
    def _(k):
        other, device = plane(k)
        remote(psend.at[other], precv.at[rows(c * tn + t, 16), :], 1, device).start()

    share_g = remote(g_hbm.at[:, cols(o, LANES)], gh_v.at[c], 2, partner)
    share_g.start()
    share_f = remote(f_hbm.at[:, cols(o, LANES)], fh_v.at[c], 3, partner)
    share_f.start()

    loads[1].wait()
    share_a.wait()
    p_all = precv.at[pl.ds(0, (2 * tn - 1) * 16), :]
    wait_bytes(p_all, recv.at[1])

    lhs = jnp.concatenate([precv[:tn * 16, :], precv[tn * 16:, :]], axis=1)
    step = min(512, quarter)
    for j in range(quarter // step):
        at = slice(j * step, (j + 1) * step)
        part = dot(lhs, a_v[:, at], NN)
        for gx in range(nx):
            for gy in range(ny):
                g = gx * ny + gy
                la[gx, gy, :, at] = unpair(part[g * 16:(g + 1) * 16])
    for k in range(1, nx):
        other, device = along_x(k)
        remote(la.at[other], ra.at[x], 4, device).start()
    for j in range(quarter // step):
        at = slice(j * step, (j + 1) * step)
        part = dot(lhs, a_v[:, quarter + j * step:quarter + (j + 1) * step], NN)
        for gx in range(nx):
            for gy in range(ny):
                g = gx * ny + gy
                lb[gy, gx, :, at] = unpair(part[g * 16:(g + 1) * 16])
    for k in range(1, ny):
        other, device = along_y(k)
        remote(lb.at[other], rb.at[y], 5, device).start()

    loads[2].wait()
    for h in range(2):
        lf[h] = unpair(dot(s2, f_v[h * half:(h + 1) * half, :], NT))
    share_l = remote(lf.at[o], lfr, 6, partner)
    share_l.start()

    wait_bytes(ra.at[pl.ds(0, nx - 1)], recv.at[4])
    total = la[x]
    for k in range(1, nx):
        total = total + ra[lax.rem(x + k, nx)]
    sa[...] = total
    for k in range(1, ny):
        other, device = along_y(k)
        remote(sa.at[other], r2a.at[y], 7, device).start()
    wait_bytes(rb.at[pl.ds(0, ny - 1)], recv.at[5])
    total = lb[y]
    for k in range(1, ny):
        total = total + rb[lax.rem(y + k, ny)]
    sb[...] = total
    for k in range(1, nx):
        other, device = along_x(k)
        remote(sb.at[other], r2b.at[x], 8, device).start()

    share_l.wait()
    feed = lf[c] + lfr[...]
    wait_bytes(r2a.at[pl.ds(0, ny - 1)], recv.at[7])
    total = sa[y] + feed[:, :quarter]
    for k in range(1, ny):
        total = total + r2a[lax.rem(y + k, ny)]
    for k in range(nz // 2):
        zs[k] = total[:, k * LANES:(k + 1) * LANES]
    wait_bytes(r2b.at[pl.ds(0, nx - 1)], recv.at[8])
    total = sb[x] + feed[:, quarter:]
    for k in range(1, nx):
        total = total + r2b[lax.rem(x + k, nx)]
    for k in range(nz // 2):
        zs[nz // 2 + k] = total[:, k * LANES:(k + 1) * LANES]

    zr[z] = zs[z]

    @pl.loop(1, nz)
    def _(k):
        other, device = along_z(k)
        remote(zs.at[other], zr.at[z], 9, device).start()

    wait_bytes(zr.at[pl.ds(0, nz - 1)], recv.at[9])
    total = zr[0]
    for k in range(1, nz):
        total = total + zr[k]
    full[c, z] = total

    @pl.loop(1, nz)
    def _(k):
        other, device = along_z(k)
        remote(full.at[c, z], full.at[c, z], 10, device).start()

    wait_bytes(full.at[c, pl.ds(0, nz - 1)], recv.at[10])
    share_full = remote(full.at[c], full.at[c], 11, partner)
    share_full.start()
    share_full.wait()

    v = [full[h, k] for h in range(2) for k in range(nz)]
    row = lax.broadcasted_iota(jnp.int32, (RANK, 1), 0)
    scale = jnp.zeros((RANK, 1), F32)
    for i in range(RANK):
        own = [jnp.broadcast_to(u[i:i + 1, :], u.shape) for u in v]
        prods = [a * b for a, b in zip(own, v)]
        while len(prods) > 1:
            prods = [a + b for a, b in zip(prods[::2], prods[1::2])]
        dots = jnp.sum(prods[0], axis=1, keepdims=True)
        square = dots[i:i + 1, :] + EPSILON
        scale = jnp.where(row == i, 1.0 / jnp.sqrt(square), scale)
        factor = jnp.where(row > i, dots / square, 0.0)
        v = [u - factor * a for u, a in zip(v, own)]
    for h in range(2):
        for k in range(nz):
            unit = v[h * nz + k] * scale
            basis_ref[:, (h * nz + k) * LANES:(h * nz + k + 1) * LANES] = unit
            bp[h, :, k * LANES:(k + 1) * LANES] = pair(unit)

    ball_a[x, y] = bp[c, :, :quarter]
    ball_b[x, y] = bp[c, :, quarter:]
    for k in range(1, nx):
        other, device = along_x(k)
        remote(ball_a.at[x, y], ball_a.at[x, y], 12, device).start()
    for k in range(1, ny):
        other, device = along_y(k)
        remote(ball_b.at[x, y], ball_b.at[x, y], 13, device).start()
    wait_bytes(ball_a.at[0, pl.ds(0, nx - 1)], recv.at[12])
    for k in range(1, ny):
        other, device = along_y(k)
        remote(ball_a.at[:, y], ball_a.at[:, y], 14, device).start()
    wait_bytes(ball_b.at[0, pl.ds(0, ny - 1)], recv.at[13])
    for k in range(1, nx):
        other, device = along_x(k)
        remote(ball_b.at[x], ball_b.at[x], 15, device).start()

    loads[4].wait()
    share_f.wait()
    right = dot(bp[0], fh_v[0, :half, :], NN) + dot(bp[1], fh_v[0, half:, :], NN)
    right = right + dot(bp[0], fh_v[1, :half, :], NN) + dot(bp[1], fh_v[1, half:, :], NN)

    wait_bytes(ball_a.at[:, pl.ds(0, ny - 1)], recv.at[14])
    q2 = dot(ball_a[...].reshape(tn * 16, quarter), a_v[:, :quarter], NT)
    wait_bytes(ball_b.at[pl.ds(0, nx - 1)], recv.at[15])
    q2 = q2 + dot(ball_b[...].reshape(tn * 16, quarter), a_v[:, quarter:], NT)
    for g in range(tn):
        qs[g] = unpair(q2[g * 16:(g + 1) * 16])

    qr[c * tn + t] = qs[t]

    @pl.loop(1, 2 * tn)
    def _(k):
        other, device = plane(k)
        remote(qs.at[other], qr.at[c * tn + t], 16, device).start()

    loads[3].wait()
    share_g.wait()
    wait_bytes(qr.at[pl.ds(0, 2 * tn - 1)], recv.at[16])
    parts = [pair(qr[k] + qr[tn + k]) for k in range(tn)]
    for h in range(2):
        q = jnp.concatenate([u[:, h * LANES:(h + 1) * LANES] for u in parts], axis=1)
        right = right + dot(q, gh_v[h], NN)
    cr[z] = unpair(right)

    @pl.loop(1, nz)
    def _(k):
        other, device = along_z(k)
        remote(cr.at[z], cr.at[z], 17, device).start()

    wait_bytes(cr.at[pl.ds(0, nz - 1)], recv.at[17])
    total = cr[0]
    for k in range(1, nz):
        total = total + cr[k]
    total = total * (1.0 / (2 * nz))
    cfin[...] = total
    coeffs_ref[:, cols(c, LANES)] = total
    share_c = remote(cfin, coeffs_ref.at[:, cols(c, LANES)], 18, partner)
    share_c.start()
    share_c.wait()

    wait_bytes(p_all, send.at[1])
    wait_bytes(ra.at[pl.ds(0, nx - 1)], send.at[4])
    wait_bytes(rb.at[pl.ds(0, ny - 1)], send.at[5])
    wait_bytes(r2a.at[pl.ds(0, ny - 1)], send.at[7])
    wait_bytes(r2b.at[pl.ds(0, nx - 1)], send.at[8])
    wait_bytes(zr.at[pl.ds(0, nz - 1)], send.at[9])
    wait_bytes(full.at[c, pl.ds(0, nz - 1)], send.at[10])
    wait_bytes(ball_a.at[0, pl.ds(0, nx - 1)], send.at[12])
    wait_bytes(ball_b.at[0, pl.ds(0, ny - 1)], send.at[13])
    wait_bytes(ball_a.at[:, pl.ds(0, ny - 1)], send.at[14])
    wait_bytes(ball_b.at[pl.ds(0, nx - 1)], send.at[15])
    wait_bytes(qr.at[pl.ds(0, 2 * tn - 1)], send.at[16])
    wait_bytes(cr.at[pl.ds(0, nz - 1)], send.at[17])


def body(nx, ny, activations, grad_query, feedback, start_factor):
    tn = nx * ny
    nz = lax.axis_size("dp") // 2
    d = activations.shape[1]
    half, quarter = d // 2, d // 4
    tok, width = grad_query.shape
    vm = pltpu.VMEM
    scratch = [
        vm((tok, width), BF16),
        vm((2 * LANES, half), BF16),
        vm((d, width), BF16),
        vm((2, tok, LANES), BF16),
        vm((2, d, LANES), BF16),
        vm((tn, 16, LANES), BF16),
        vm((2 * tn * 16, LANES), BF16),
        vm((nx, ny, RANK, quarter), F32),
        vm((ny, nx, RANK, quarter), F32),
        vm((nx, ny, RANK, quarter), F32),
        vm((ny, nx, RANK, quarter), F32),
        vm((ny, RANK, quarter), F32),
        vm((nx, RANK, quarter), F32),
        vm((ny, RANK, quarter), F32),
        vm((nx, RANK, quarter), F32),
        vm((2, RANK, half), F32),
        vm((RANK, half), F32),
        vm((nz, RANK, LANES), F32),
        vm((nz, RANK, LANES), F32),
        vm((2, nz, RANK, LANES), F32),
        vm((2, 16, half), BF16),
        vm((nx, ny, 16, quarter), BF16),
        vm((nx, ny, 16, quarter), BF16),
        vm((tn, RANK, 2 * LANES), F32),
        vm((2 * tn, RANK, 2 * LANES), F32),
        vm((nz, RANK, LANES), F32),
        vm((RANK, LANES), F32),
        pltpu.SemaphoreType.DMA((5,)),
        pltpu.SemaphoreType.DMA((19,)),
        pltpu.SemaphoreType.DMA((19,)),
    ]
    anywhere = pl.BlockSpec(memory_space=pl.ANY)
    inside = pl.BlockSpec(memory_space=pltpu.VMEM)
    return pl.pallas_call(
        functools.partial(kernel, nx, ny, nz),
        out_shape=(
            jax.ShapeDtypeStruct((RANK, d), F32),
            jax.ShapeDtypeStruct((RANK, width), F32),
        ),
        in_specs=[inside, anywhere, anywhere, anywhere],
        out_specs=(inside, inside),
        scratch_shapes=scratch,
        compiler_params=pltpu.CompilerParams(
            collective_id=0, has_side_effects=True, vmem_limit_bytes=48 * 1024 * 1024
        ),
    )(start_factor, grad_query, activations, feedback)


def solution(mesh):
    side = 4 if mesh.shape["tensor"] == 16 else 2
    in_specs = (P(("dp", "tensor"), None), P("dp", "tensor"), P("dp", "tensor"), P(None, "tensor"))
    out_specs = (P("tensor", None), P(None, "tensor"))
    return jax.shard_map(
        functools.partial(body, side, mesh.shape["tensor"] // side),
        mesh=mesh, in_specs=in_specs, out_specs=out_specs, check_vma=False,
    )
```

time: 485 us -> 87.7 us (0.18)
  waiting for transfers between devices: 331 us -> 0 us
  Pallas kernels: 0 us -> 80.8 us
  other arithmetic: 62.6 us -> 0 us
  blocking collectives: 46.7 us -> 0 us
  matrix products: 19.8 us -> 0 us
  between operations: 19.5 us -> 0.65 us
    psum x1 -> x0, waiting for transfers between devices: 196 us -> none  [body(): summed_left = lax.psum(local_left, 'dp')]
    all_gather x1 -> x0, waiting for transfers between devices: 135 us -> none  [body(): lax.all_gather(activations, 'tensor', axis=0, tiled=True)]
    pallas_call x0 -> x1, Pallas kernels: none -> 80.8 us  [body(): pl.pallas_call(functools.partial(kernel, nx, ny, nz), out_shape=(jax.Shap...]
    psum x1 -> x0, blocking collectives: 46.7 us -> none  [body(): coeffs = lax.psum(local_right, 'dp') / replicas]
    reduce_sum x15 -> x0, other arithmetic: 41 us -> none  [the longest x10 31.2 us: orthonormal_rows(): vector = vector - jnp.sum(earlier * vector) * earlier]
    div x2 -> x0, other arithmetic: 19.9 us -> none  [the longest x1 19.3 us: orthonormal_rows(): vector = vector / jnp.sqrt(jnp.sum(vector * vector) + EPSILON)]
    dot_general x5 -> x0, matrix products: 19.8 us -> none  [the longest x1 8.89 us: body(): lax.dot_general(lax.all_gather(activations, 'tensor', axis=0, tiled=True)...]
  transfers between devices with their start and end apart: 2 -> 0, of which waited for: 2 -> 0; matrix products, arithmetic and copies ran while one was open for 0% -> 0% of each run, Pallas kernels for 0% -> 0%
where the time goes in v1:
time: 87.7 us; the launch traced here: 87.4 us
  Pallas kernels  80.8 us (92%)
  local copies, waits for them, and re-layouts  5.98 us (7%)
    pallas_call x1, Pallas kernels, body(): pl.pallas_call(functools.partial(kernel, nx, ny, nz), out_shape=(jax.Shap...  80.8 us
    unnamed x10, local copies, waits for them, and re-layouts  5.98 us

profile of v1, /device:TPU:1, one launch (start us, length us, event | category | flops | bytes accessed | tf_op | source)
XLA Modules:
  0.0 87.4 jit_solution(16731078891608698376)
XLA Ops:
  0.6 0.0 copy-start
  0.6 1.6 %copy-done = bf16[4096,256]{1,0:T(8,128)(2,1)S(1)} copy-done((bf16[4096,256]{1,0:T(8,128)(2,1)S(1)}, bf16[4096,256]{1,0:T(8,128)(2,1)}, u32[]{:S(2)}) %copy-start) | copy-done | bytes 2097176
  2.2 0.0 copy-start.1
  2.2 1.2 %copy-done.1 = bf16[2048,256]{1,0:T(8,128)(2,1)S(1)} copy-done((bf16[2048,256]{1,0:T(8,128)(2,1)S(1)}, bf16[2048,256]{1,0:T(8,128)(2,1)}, u32[]{:S(2)}) %copy-start.1) | copy-done | bytes 1048600
  3.4 0.0 copy-start.2
  3.5 1.2 %copy-done.2 = bf16[128,4096]{1,0:T(8,128)(2,1)S(1)} copy-done((bf16[128,4096]{1,0:T(8,128)(2,1)S(1)}, bf16[128,4096]{1,0:T(8,128)(2,1)}, u32[]{:S(2)}) %copy-start.2) | copy-done | bytes 1048600
  4.7 0.0 copy-start.3
  4.7 0.7 copy-done.3
  5.4 80.8 %shard_map.59 = (f32[8,4096]{1,0:T(8,128)S(1)}, f32[8,256]{1,0:T(8,128)S(1)}) custom-call(f32[8,256]{1,0:T(8,128)S(1)} %copy-done.3, bf16[2048,256]{1,0:T(8,128)(2,1)S(1)} %copy-done.1, bf16[128,4096]{1,0:T(8,128)(2,1)S(1)} %copy-done.2, bf16[4096,256]{1,0:T(8,128)(2,1)S(1)} %copy-done), custom_call_target="tpu_custom_call" | custom-call | tf_op jit(solution)/shard_map/pallas_call | solution.py:354
  86.2 0.7 copy.8
  86.8 0.6 copy.9
Async XLA Ops:
  0.6 1.6 %copy-start = (bf16[4096,256]{1,0:T(8,128)(2,1)S(1)}, bf16[4096,256]{1,0:T(8,128)(2,1)}, u32[]{:S(2)}) copy-start(bf16[4096,256]{1,0:T(8,128)(2,1)} %f_hbm.1) | copy-start | bytes 6291460
  2.2 1.2 %copy-start.1 = (bf16[2048,256]{1,0:T(8,128)(2,1)S(1)}, bf16[2048,256]{1,0:T(8,128)(2,1)}, u32[]{:S(2)}) copy-start(bf16[2048,256]{1,0:T(8,128)(2,1)} %g_hbm.1) | copy-start | bytes 3145732
  3.4 1.2 %copy-start.2 = (bf16[128,4096]{1,0:T(8,128)(2,1)S(1)}, bf16[128,4096]{1,0:T(8,128)(2,1)}, u32[]{:S(2)}) copy-start(bf16[128,4096]{1,0:T(8,128)(2,1)} %a_hbm.1) | copy-start | bytes 3145732
  4.7 0.7 copy-start.3

commit v2 on v0

v2 whole, which is shorter than its diff:
```python
import functools
import itertools

import jax
import jax.numpy as jnp
from jax import lax
from jax.experimental import pallas as pl
from jax.experimental.pallas import tpu as pltpu
from jax.sharding import PartitionSpec as P

EPSILON = 1e-06
MESH = pl.DeviceIdType.MESH
F32, BF16 = jnp.float32, jnp.bfloat16
RANK = 8
LANES = 128
NT = (((1,), (1,)), ((), ()))
NN = (((1,), (0,)), ((), ()))
NEAR_A, FAR_A, FAR_B, NEAR_B = range(4)
CHANNELS = 48


def dot(a, b, dims):
    return lax.dot_general(a, b, dims, preferred_element_type=F32)


def pair(value):
    top = value.astype(BF16).astype(F32)
    return jnp.concatenate([top, value - top], axis=0).astype(BF16)


def unpair(value):
    return value[:RANK] + value[RANK:]


def wait_bytes(ref, sem):
    pltpu.make_async_copy(ref, ref, sem).wait()


def hops(k, n):
    return min(k, n - k)


def kernel(
    nx, ny, nz,
    s_hbm, g_hbm, a_hbm, f_hbm,
    basis_hbm, coeffs_ref,
    s_v, g_v, a_v, f_v, gh_v, fh_v,
    psend, precv,
    first, first_in, second, second_in,
    lf, lfr, zs, zr,
    ball, other_half, basis_v, qacc,
    qs, qr, cr, cfin,
    local, send, recv, ready,
):
    tn = nx * ny
    half = a_v.shape[1]
    slots = nz // 4
    dp, t = lax.axis_index("dp"), lax.axis_index("tensor")
    z, c = dp // 2, lax.rem(dp, 2)
    o = 1 - c
    x, y = t // ny, lax.rem(t, ny)
    partner = (2 * z + o, t)
    xs = [x] + [lax.rem(x + k, nx) for k in range(1, nx)]
    ys = [y] + [lax.rem(y + k, ny) for k in range(1, ny)]
    around = [z] + [lax.rem(z + k, nz) for k in range(1, nz)]

    def block(index, size):
        return pl.ds(pl.multiple_of(index * size, size), size)

    counter = itertools.count()
    sent = []

    def remote(src, dst, channel, device):
        return pltpu.make_async_remote_copy(
            src_ref=src, dst_ref=dst, send_sem=send.at[channel], recv_sem=recv.at[channel],
            device_id=device, device_id_type=MESH,
        )

    def arrived(ref, channel):
        wait_bytes(ref, recv.at[channel])
        sent.append((ref, channel))

    def along_z(k):
        return (2 * around[k] + c, t)

    def along_x(k):
        return (dp, xs[k] * ny + y)

    def along_y(k):
        return (dp, x * ny + ys[k])

    plane = []
    for dx, dy, dc in itertools.product(range(nx), range(ny), range(2)):
        if dx + dy + dc:
            group = xs[dx] * ny + ys[dy]
            plane.append((hops(dx, nx) + hops(dy, ny), group, (2 * z + o if dc else dp, group)))
    plane.sort(key=lambda entry: -entry[0])
    by_distance = sorted(range(1, nz), key=lambda k: -hops(k, nz))

    load_s = pltpu.make_async_copy(s_hbm, s_v, local.at[0])
    load_g = pltpu.make_async_copy(g_hbm, g_v, local.at[1])
    load_a = pltpu.make_async_copy(a_hbm.at[:, block(c, half)], a_v.at[block(c, LANES), :], local.at[2])
    load_f = pltpu.make_async_copy(f_hbm, f_v, local.at[3])
    load_gh = pltpu.make_async_copy(g_hbm.at[:, block(c, LANES)], gh_v.at[c], local.at[4])
    load_fh = pltpu.make_async_copy(f_hbm.at[:, block(c, LANES)], fh_v.at[c], local.at[5])
    load_s.start()
    load_g.start()

    barrier = pltpu.get_barrier_semaphore()
    beside = sorted({1, nz - 1})
    for _, _, device in plane:
        pl.semaphore_signal(barrier, inc=1, device_id=device, device_id_type=MESH)
    for k in beside:
        pl.semaphore_signal(barrier, inc=1, device_id=along_z(k), device_id_type=MESH)
    for load in (load_a, load_f, load_gh, load_fh):
        load.start()

    reach = [2 ** k for k in range(8) if 2 ** k < nz // 2]

    def tell(step):
        for k in (reach[step], nz - reach[step]):
            pl.semaphore_signal(ready.at[step], inc=1, device_id=along_z(k), device_id_type=MESH)

    load_s.wait()
    s2 = pair(s_v[...])
    load_g.wait()
    p2 = pair(unpair(dot(s2, g_v[...], NT)))
    for k in range(tn):
        psend[k] = p2[:, k * LANES:(k + 1) * LANES]

    pl.semaphore_wait(barrier, len(plane) + len(beside))

    p_channel = next(counter)
    for _, group, device in plane:
        remote(psend.at[group], precv.at[block(c * tn + t, 16), :], p_channel, device).start()
    share_a = remote(a_hbm.at[:, block(o, half)], a_v.at[block(c, LANES), :], next(counter), partner)
    share_a.start()
    tell(0)
    precv[block(c * tn + t, 16), :] = psend[t]
    share_g = remote(g_hbm.at[:, block(o, LANES)], gh_v.at[c], next(counter), partner)
    share_g.start()
    share_f = remote(f_hbm.at[:, block(o, LANES)], fh_v.at[c], next(counter), partner)
    share_f.start()

    load_a.wait()
    share_a.wait()
    arrived(precv.at[pl.ds(0, (2 * tn - 1) * 16), :], p_channel)

    def features(k):
        return a_v[:, block(around[k], LANES)]

    def region(r):
        return range(r * slots, (r + 1) * slots)

    def order(r):
        on_x, on_y = (x, nx, xs, along_x), (y, ny, ys, along_y)
        return (on_x, on_y) if r in (NEAR_A, FAR_A) else (on_y, on_x)

    lhs = jnp.concatenate([precv[:tn * 16, :], precv[tn * 16:, :]], axis=1)
    first_channel, second_channel = {}, {}
    for r in (FAR_A, FAR_B, NEAR_A, NEAR_B):
        (here, count, _, device), _ = order(r)
        part = dot(lhs, jnp.concatenate([features(k) for k in region(r)], axis=1), NN)
        for gx in range(nx):
            for gy in range(ny):
                g = gx * ny + gy
                i, j = (gx, gy) if r in (NEAR_A, FAR_A) else (gy, gx)
                first[r, i, j] = unpair(part[g * 16:(g + 1) * 16])
        first_channel[r] = next(counter)
        others = order(r)[0][2]
        for k in range(1, count):
            remote(first.at[r, others[k]], first_in.at[r, here], first_channel[r], device(k)).start()
    if len(reach) > 1:
        pl.semaphore_wait(ready.at[0], 2)
        tell(1)

    load_f.wait()
    for h in range(2):
        for k in range(nz):
            at = (h * nz + k) * LANES
            lf[h, k] = unpair(dot(s2, f_v[at:at + LANES, :], NT))
    share_l = remote(lf.at[o], lfr, next(counter), partner)
    share_l.start()

    for r in (FAR_A, FAR_B, NEAR_A, NEAR_B):
        (here, count, others, _), (place, size, beyond, device) = order(r)
        arrived(first_in.at[r, pl.ds(0, count - 1)], first_channel[r])
        total = first[r, here]
        for k in range(1, count):
            total = total + first_in[r, others[k]]
        second[r] = total
        second_channel[r] = next(counter)
        for k in range(1, size):
            remote(second.at[r, beyond[k]], second_in.at[r, place], second_channel[r], device(k)).start()
    if len(reach) > 2:
        pl.semaphore_wait(ready.at[1], 2)
        tell(2)

    share_l.wait()
    z_channel = next(counter)
    for r in (FAR_A, FAR_B, NEAR_A, NEAR_B):
        _, (place, size, beyond, _) = order(r)
        arrived(second_in.at[r, pl.ds(0, size - 1)], second_channel[r])
        total = second[r, place]
        for k in range(1, size):
            total = total + second_in[r, beyond[k]]
        for i, k in enumerate(region(r)):
            zs[k] = total[:, i * LANES:(i + 1) * LANES] + (lf[c, around[k]] + lfr[around[k]])
        if r == FAR_A:
            for step in range(max(len(reach) - 1, 0), len(reach)):
                pl.semaphore_wait(ready.at[step], 2)
        for k in sorted(region(r), key=lambda k: -hops(k, nz)):
            if k:
                remote(zs.at[k], zr.at[k], z_channel, along_z(k)).start()
    arrived(zr.at[pl.ds(0, nz - 1)], z_channel)
    total = zs[0]
    for k in range(1, nz):
        total = total + zr[k]

    ball[x, y, 0] = pair(total)
    gather = [next(counter) for _ in range(4)]
    for k in by_distance:
        remote(ball.at[x, y, 0], ball.at[x, y, k], gather[k // slots], along_z(nz - k)).start()

    def part_of(r):
        return pl.ds(r * slots, slots)

    def spread_own(r):
        own = part_of(r)
        if r == NEAR_A:
            if slots > 1:
                arrived(ball.at[x, y, pl.ds(0, slots - 1)], gather[r])
        else:
            arrived(ball.at[x, y, own], gather[r])
        first_channel[r] = next(counter)
        (_, count, _, device), _ = order(r)
        for k in range(1, count):
            remote(ball.at[x, y, own], ball.at[x, y, own], first_channel[r], device(k)).start()

    def spread_line(r):
        own = part_of(r)
        (_, count, _, _), (_, size, _, device) = order(r)
        arrived(ball.at[x, pl.ds(0, count - 1), own], first_channel[r])
        second_channel[r] = next(counter)
        line = ball.at[:, y, own] if r in (NEAR_A, FAR_A) else ball.at[x, :, own]
        for k in range(1, size):
            remote(line, line, second_channel[r], device(k)).start()

    def product(r):
        own = part_of(r)
        _, (_, size, _, _) = order(r)
        rest = ball.at[:, pl.ds(0, size - 1), own] if r in (NEAR_A, FAR_A) else ball.at[pl.ds(0, size - 1), :, own]
        arrived(rest, second_channel[r])
        left = jnp.concatenate([ball[:, :, k].reshape(tn * 16, LANES) for k in region(r)], axis=1)
        return dot(left, jnp.concatenate([features(k) for k in region(r)], axis=1), NT)

    spread_own(NEAR_A)
    spread_own(NEAR_B)
    spread_line(NEAR_A)
    spread_line(NEAR_B)
    spread_own(FAR_A)
    spread_own(FAR_B)
    share_half = remote(ball.at[x, y], other_half, next(counter), partner)
    share_half.start()
    qacc[...] = product(NEAR_A) + product(NEAR_B)
    spread_line(FAR_A)
    spread_line(FAR_B)

    share_half.wait()
    pairs = []
    for h in range(2):
        for k in range(nz):
            slot = lax.rem(k - z + nz, nz)
            pairs.append(jnp.where(c == h, ball[x, y, slot].astype(F32), other_half[slot].astype(F32)))
    v = [unpair(u) for u in pairs]
    row = lax.broadcasted_iota(jnp.int32, (RANK, 1), 0)
    ops = (lax.broadcasted_iota(jnp.int32, (RANK, LANES), 0) == lax.broadcasted_iota(jnp.int32, (RANK, LANES), 1)).astype(F32)
    scale = jnp.zeros((RANK, 1), F32)
    for i in range(RANK):
        own = [jnp.broadcast_to(u[i:i + 1, :], u.shape) for u in v]
        prods = [a * b for a, b in zip(own, v)]
        while len(prods) > 1:
            prods = [a + b for a, b in zip(prods[::2], prods[1::2])]
        dots = jnp.sum(prods[0], axis=1, keepdims=True)
        square = dots[i:i + 1, :] + EPSILON
        scale = jnp.where(row == i, 1.0 / jnp.sqrt(square), scale)
        factor = jnp.where(row > i, dots / square, 0.0)
        v = [u - factor * a for u, a in zip(v, own)]
        ops = ops - factor * jnp.broadcast_to(ops[i:i + 1, :], ops.shape)
    ops = ops * scale
    for k, u in enumerate(v):
        basis_v[:, k * LANES:(k + 1) * LANES] = u * scale
    store_basis = pltpu.make_async_copy(basis_v, basis_hbm, local.at[6])
    store_basis.start()

    load_fh.wait()
    share_f.wait()
    left = jnp.concatenate([u.astype(BF16) for u in pairs], axis=1)
    right = dot(left, fh_v[0], NN) + dot(left, fh_v[1], NN)

    q2 = qacc[...] + product(FAR_A) + product(FAR_B)
    for g in range(tn):
        qs[g] = unpair(q2[g * 16:(g + 1) * 16])
    q_channel = next(counter)
    for _, group, device in plane:
        remote(qs.at[group], qr.at[c * tn + t], q_channel, device).start()
    qr[c * tn + t] = qs[t]

    load_gh.wait()
    share_g.wait()
    arrived(qr.at[pl.ds(0, 2 * tn - 1)], q_channel)
    parts = [pair(qr[k] + qr[tn + k]) for k in range(tn)]
    for h in range(2):
        q = jnp.concatenate([u[:, h * LANES:(h + 1) * LANES] for u in parts], axis=1)
        right = right + dot(q, gh_v[h], NN)
    right = unpair(right)
    cr[z] = sum(ops[:, i:i + 1] * right[i:i + 1, :] for i in range(RANK))

    c_channel = next(counter)
    for k in by_distance:
        remote(cr.at[z], cr.at[z], c_channel, along_z(k)).start()
    arrived(cr.at[pl.ds(0, nz - 1)], c_channel)
    total = cr[0]
    for k in range(1, nz):
        total = total + cr[k]
    total = total * (1.0 / (2 * nz))
    cfin[...] = total
    coeffs_ref[:, block(c, LANES)] = total
    share_c = remote(cfin, coeffs_ref.at[:, block(c, LANES)], next(counter), partner)
    share_c.start()

    store_basis.wait()
    for ref, channel in sent:
        wait_bytes(ref, send.at[channel])
    share_c.wait()


def body(nx, ny, activations, grad_query, feedback, start_factor):
    tn = nx * ny
    nz = lax.axis_size("dp") // 2
    d = activations.shape[1]
    half, quarter = d // 2, d // 8
    tok, width = grad_query.shape
    vm = pltpu.VMEM
    side = max(nx, ny)
    scratch = [
        vm((RANK, width), F32),
        vm((tok, width), BF16),
        vm((2 * LANES, half), BF16),
        vm((d, width), BF16),
        vm((2, tok, LANES), BF16),
        vm((2, d, LANES), BF16),
        vm((tn, 16, LANES), BF16),
        vm((2 * tn * 16, LANES), BF16),
        vm((4, side, side, RANK, quarter), F32),
        vm((4, side, side, RANK, quarter), F32),
        vm((4, side, RANK, quarter), F32),
        vm((4, side, RANK, quarter), F32),
        vm((2, nz, RANK, LANES), F32),
        vm((nz, RANK, LANES), F32),
        vm((nz, RANK, LANES), F32),
        vm((nz, RANK, LANES), F32),
        vm((nx, ny, nz, 16, LANES), BF16),
        vm((nz, 16, LANES), BF16),
        vm((RANK, d), F32),
        vm((tn * 16, 2 * LANES), F32),
        vm((tn, RANK, 2 * LANES), F32),
        vm((2 * tn, RANK, 2 * LANES), F32),
        vm((nz, RANK, LANES), F32),
        vm((RANK, LANES), F32),
        pltpu.SemaphoreType.DMA((7,)),
        pltpu.SemaphoreType.DMA((CHANNELS,)),
        pltpu.SemaphoreType.DMA((CHANNELS,)),
        pltpu.SemaphoreType.REGULAR((4,)),
    ]
    anywhere = pl.BlockSpec(memory_space=pl.ANY)
    return pl.pallas_call(
        functools.partial(kernel, nx, ny, nz),
        out_shape=(
            jax.ShapeDtypeStruct((RANK, d), F32),
            jax.ShapeDtypeStruct((RANK, width), F32),
        ),
        in_specs=[anywhere] * 4,
        out_specs=(anywhere, pl.BlockSpec(memory_space=pltpu.VMEM)),
        scratch_shapes=scratch,
        compiler_params=pltpu.CompilerParams(
            collective_id=0, has_side_effects=True, vmem_limit_bytes=60 * 1024 * 1024
        ),
    )(start_factor, grad_query, activations, feedback)


def solution(mesh):
    side = 4 if mesh.shape["tensor"] == 16 else 2
    in_specs = (P(("dp", "tensor"), None), P("dp", "tensor"), P("dp", "tensor"), P(None, "tensor"))
    out_specs = (P("tensor", None), P(None, "tensor"))
    return jax.shard_map(
        functools.partial(body, side, mesh.shape["tensor"] // side),
        mesh=mesh, in_specs=in_specs, out_specs=out_specs, check_vma=False,
    )
```

time: 485 us -> 79.8 us (0.16)
  waiting for transfers between devices: 331 us -> 0 us
  Pallas kernels: 0 us -> 76 us
  other arithmetic: 62.6 us -> 0 us
  blocking collectives: 46.7 us -> 0 us
  matrix products: 19.8 us -> 0 us
  between operations: 19.5 us -> 0.64 us
    psum x1 -> x0, waiting for transfers between devices: 196 us -> none  [body(): summed_left = lax.psum(local_left, 'dp')]
    all_gather x1 -> x0, waiting for transfers between devices: 135 us -> none  [body(): lax.all_gather(activations, 'tensor', axis=0, tiled=True)]
    pallas_call x0 -> x1, Pallas kernels: none -> 76 us  [body(): pl.pallas_call(functools.partial(kernel, nx, ny, nz), out_shape=(jax.Shap...]
    psum x1 -> x0, blocking collectives: 46.7 us -> none  [body(): coeffs = lax.psum(local_right, 'dp') / replicas]
    reduce_sum x15 -> x0, other arithmetic: 41 us -> none  [the longest x10 31.2 us: orthonormal_rows(): vector = vector - jnp.sum(earlier * vector) * earlier]
    div x2 -> x0, other arithmetic: 19.9 us -> none  [the longest x1 19.3 us: orthonormal_rows(): vector = vector / jnp.sqrt(jnp.sum(vector * vector) + EPSILON)]
    dot_general x5 -> x0, matrix products: 19.8 us -> none  [the longest x1 8.89 us: body(): lax.dot_general(lax.all_gather(activations, 'tensor', axis=0, tiled=True)...]
  transfers between devices with their start and end apart: 2 -> 0, of which waited for: 2 -> 0; matrix products, arithmetic and copies ran while one was open for 0% -> 0% of each run, Pallas kernels for 0% -> 0%
where the time goes in v2:
time: 79.8 us; the launch traced here: 79.5 us
  Pallas kernels  76 us (95%)
  local copies, waits for them, and re-layouts  2.86 us (4%)
    pallas_call x1, Pallas kernels, body(): pl.pallas_call(functools.partial(kernel, nx, ny, nz), out_shape=(jax.Shap...  76 us
    unnamed x2, local copies, waits for them, and re-layouts  2.86 us

profile of v2, /device:TPU:1, one launch (start us, length us, event | category | flops | bytes accessed | tf_op | source)
XLA Modules:
  0.0 79.5 jit_solution(19778533622928040)
XLA Ops:
  0.6 76.0 %shard_map.59 = (f32[8,4096]{1,0:T(8,128)}, f32[8,256]{1,0:T(8,128)}) custom-call(f32[8,256]{1,0:T(8,128)} %s_hbm.1, bf16[2048,256]{1,0:T(8,128)(2,1)} %g_hbm.1, bf16[128,4096]{1,0:T(8,128)(2,1)} %a_hbm.1, bf16[4096,256]{1,0:T(8,128)(2,1)} %f_hbm.1), custom_call_target="tpu_custom_call" | custom-call | tf_op jit(solution)/shard_map/pallas_call | solution.py:377
  76.7 1.6 %copy.8 = f32[8,4096]{1,0:T(8,128)} copy(f32[8,4096]{1,0:T(8,128)} %get-tuple-element.4) | data formatting | bytes 262144
  78.2 1.3 %copy.9 = f32[8,256]{1,0:T(8,128)} copy(f32[8,256]{1,0:T(8,128)} %get-tuple-element.5) | data formatting | bytes 16384

commit v3 on v2

--- a/solution.py
+++ b/solution.py
@@ -15,8 +15,7 @@
 LANES = 128
 NT = (((1,), (1,)), ((), ()))
 NN = (((1,), (0,)), ((), ()))
-NEAR_A, FAR_A, FAR_B, NEAR_B = range(4)
-CHANNELS = 48
+CHANNELS = 56
 
 
 def dot(a, b, dims):
@@ -48,13 +47,14 @@
     psend, precv,
     first, first_in, second, second_in,
     lf, lfr, zs, zr,
-    ball, other_half, basis_v, qacc,
+    ball, other_half, basis_v,
     qs, qr, cr, cfin,
     local, send, recv, ready,
 ):
     tn = nx * ny
     half = a_v.shape[1]
-    slots = nz // 4
+    slots = max(nz // 8, 1)
+    groups = nz // (2 * slots)
     dp, t = lax.axis_index("dp"), lax.axis_index("tensor")
     z, c = dp // 2, lax.rem(dp, 2)
     o = 1 - c
@@ -137,10 +137,6 @@
     share_a.start()
     tell(0)
     precv[block(c * tn + t, 16), :] = psend[t]
-    share_g = remote(g_hbm.at[:, block(o, LANES)], gh_v.at[c], next(counter), partner)
-    share_g.start()
-    share_f = remote(f_hbm.at[:, block(o, LANES)], fh_v.at[c], next(counter), partner)
-    share_f.start()
 
     load_a.wait()
     share_a.wait()
@@ -149,27 +145,39 @@
     def features(k):
         return a_v[:, block(around[k], LANES)]
 
+    def start(r):
+        return r[0] * slots if r[1] == 0 else nz - (r[0] + 1) * slots
+
     def region(r):
-        return range(r * slots, (r + 1) * slots)
+        return range(start(r), start(r) + slots)
 
     def order(r):
         on_x, on_y = (x, nx, xs, along_x), (y, ny, ys, along_y)
-        return (on_x, on_y) if r in (NEAR_A, FAR_A) else (on_y, on_x)
+        return (on_y, on_x) if r[1] else (on_x, on_y)
+
+    def part_of(r):
+        return pl.ds(start(r), slots)
+
+    def index(r):
+        return 2 * r[0] + r[1]
+
+    nearest = [(i, side) for i in range(groups) for side in range(2)]
+    farthest = [(i, side) for i in reversed(range(groups)) for side in range(2)]
 
     lhs = jnp.concatenate([precv[:tn * 16, :], precv[tn * 16:, :]], axis=1)
     first_channel, second_channel = {}, {}
-    for r in (FAR_A, FAR_B, NEAR_A, NEAR_B):
+    for r in farthest:
         (here, count, _, device), _ = order(r)
         part = dot(lhs, jnp.concatenate([features(k) for k in region(r)], axis=1), NN)
         for gx in range(nx):
             for gy in range(ny):
                 g = gx * ny + gy
-                i, j = (gx, gy) if r in (NEAR_A, FAR_A) else (gy, gx)
-                first[r, i, j] = unpair(part[g * 16:(g + 1) * 16])
+                i, j = (gy, gx) if r[1] else (gx, gy)
+                first[index(r), i, j] = unpair(part[g * 16:(g + 1) * 16])
         first_channel[r] = next(counter)
         others = order(r)[0][2]
         for k in range(1, count):
-            remote(first.at[r, others[k]], first_in.at[r, here], first_channel[r], device(k)).start()
+            remote(first.at[index(r), others[k]], first_in.at[index(r), here], first_channel[r], device(k)).start()
     if len(reach) > 1:
         pl.semaphore_wait(ready.at[0], 2)
         tell(1)
@@ -182,52 +190,62 @@
     share_l = remote(lf.at[o], lfr, next(counter), partner)
     share_l.start()
 
-    for r in (FAR_A, FAR_B, NEAR_A, NEAR_B):
+    def pass_on(r):
         (here, count, others, _), (place, size, beyond, device) = order(r)
-        arrived(first_in.at[r, pl.ds(0, count - 1)], first_channel[r])
-        total = first[r, here]
+        arrived(first_in.at[index(r), pl.ds(0, count - 1)], first_channel[r])
+        total = first[index(r), here]
         for k in range(1, count):
-            total = total + first_in[r, others[k]]
-        second[r] = total
+            total = total + first_in[index(r), others[k]]
+        second[index(r)] = total
         second_channel[r] = next(counter)
         for k in range(1, size):
-            remote(second.at[r, beyond[k]], second_in.at[r, place], second_channel[r], device(k)).start()
+            remote(second.at[index(r), beyond[k]], second_in.at[index(r), place], second_channel[r], device(k)).start()
+
+    z_channel = next(counter)
+
+    def pass_along_z(r):
+        _, (place, size, beyond, _) = order(r)
+        arrived(second_in.at[index(r), pl.ds(0, size - 1)], second_channel[r])
+        total = second[index(r), place]
+        for k in range(1, size):
+            total = total + second_in[index(r), beyond[k]]
+        for i, k in enumerate(region(r)):
+            zs[k] = total[:, i * LANES:(i + 1) * LANES] + (lf[c, around[k]] + lfr[around[k]])
+        for k in sorted(region(r), key=lambda k: -hops(k, nz)):
+            if k:
+                remote(zs.at[k], zr.at[k], z_channel, along_z(k)).start()
+
+    ahead = len(farthest) - 2
+    for r in farthest[:ahead]:
+        pass_on(r)
     if len(reach) > 2:
         pl.semaphore_wait(ready.at[1], 2)
         tell(2)
-
     share_l.wait()
-    z_channel = next(counter)
-    for r in (FAR_A, FAR_B, NEAR_A, NEAR_B):
-        _, (place, size, beyond, _) = order(r)
-        arrived(second_in.at[r, pl.ds(0, size - 1)], second_channel[r])
-        total = second[r, place]
-        for k in range(1, size):
-            total = total + second_in[r, beyond[k]]
-        for i, k in enumerate(region(r)):
-            zs[k] = total[:, i * LANES:(i + 1) * LANES] + (lf[c, around[k]] + lfr[around[k]])
-        if r == FAR_A:
-            for step in range(max(len(reach) - 1, 0), len(reach)):
-                pl.semaphore_wait(ready.at[step], 2)
-        for k in sorted(region(r), key=lambda k: -hops(k, nz)):
-            if k:
-                remote(zs.at[k], zr.at[k], z_channel, along_z(k)).start()
+    for step in range(max(len(reach) - 1, 0), len(reach)):
+        pl.semaphore_wait(ready.at[step], 2)
+    for r, late in itertools.zip_longest(farthest, farthest[ahead:]):
+        pass_along_z(r)
+        if late:
+            pass_on(late)
+    share_g = remote(g_hbm.at[:, block(o, LANES)], gh_v.at[c], next(counter), partner)
+    share_g.start()
+    share_f = remote(f_hbm.at[:, block(o, LANES)], fh_v.at[c], next(counter), partner)
+    share_f.start()
     arrived(zr.at[pl.ds(0, nz - 1)], z_channel)
     total = zs[0]
     for k in range(1, nz):
         total = total + zr[k]
 
     ball[x, y, 0] = pair(total)
-    gather = [next(counter) for _ in range(4)]
+    gather = {r: next(counter) for r in nearest}
     for k in by_distance:
-        remote(ball.at[x, y, 0], ball.at[x, y, k], gather[k // slots], along_z(nz - k)).start()
-
-    def part_of(r):
-        return pl.ds(r * slots, slots)
+        r = next(r for r in nearest if k in region(r))
+        remote(ball.at[x, y, 0], ball.at[x, y, k], gather[r], along_z(nz - k)).start()
 
     def spread_own(r):
         own = part_of(r)
-        if r == NEAR_A:
+        if r == nearest[0]:
             if slots > 1:
                 arrived(ball.at[x, y, pl.ds(0, slots - 1)], gather[r])
         else:
@@ -242,29 +260,28 @@
         (_, count, _, _), (_, size, _, device) = order(r)
         arrived(ball.at[x, pl.ds(0, count - 1), own], first_channel[r])
         second_channel[r] = next(counter)
-        line = ball.at[:, y, own] if r in (NEAR_A, FAR_A) else ball.at[x, :, own]
+        line = ball.at[:, y, own] if r[1] == 0 else ball.at[x, :, own]
         for k in range(1, size):
             remote(line, line, second_channel[r], device(k)).start()
 
     def product(r):
         own = part_of(r)
         _, (_, size, _, _) = order(r)
-        rest = ball.at[:, pl.ds(0, size - 1), own] if r in (NEAR_A, FAR_A) else ball.at[pl.ds(0, size - 1), :, own]
+        rest = ball.at[:, pl.ds(0, size - 1), own] if r[1] == 0 else ball.at[pl.ds(0, size - 1), :, own]
         arrived(rest, second_channel[r])
         left = jnp.concatenate([ball[:, :, k].reshape(tn * 16, LANES) for k in region(r)], axis=1)
         return dot(left, jnp.concatenate([features(k) for k in region(r)], axis=1), NT)
 
-    spread_own(NEAR_A)
-    spread_own(NEAR_B)
-    spread_line(NEAR_A)
-    spread_line(NEAR_B)
-    spread_own(FAR_A)
-    spread_own(FAR_B)
-    share_half = remote(ball.at[x, y], other_half, next(counter), partner)
-    share_half.start()
-    qacc[...] = product(NEAR_A) + product(NEAR_B)
-    spread_line(FAR_A)
-    spread_line(FAR_B)
+    for step in range(groups + 2):
+        if step < groups:
+            spread_own((step, 0))
+            spread_own((step, 1))
+        if step >= 2:
+            spread_line((step - 2, 0))
+            spread_line((step - 2, 1))
+        if step == groups - 1:
+            share_half = remote(ball.at[x, y], other_half, next(counter), partner)
+            share_half.start()
 
     share_half.wait()
     pairs = []
@@ -298,7 +315,7 @@
     left = jnp.concatenate([u.astype(BF16) for u in pairs], axis=1)
     right = dot(left, fh_v[0], NN) + dot(left, fh_v[1], NN)
 
-    q2 = qacc[...] + product(FAR_A) + product(FAR_B)
+    q2 = sum(product(r) for r in nearest)
     for g in range(tn):
         qs[g] = unpair(q2[g * 16:(g + 1) * 16])
     q_channel = next(counter)
@@ -339,7 +356,9 @@
     tn = nx * ny
     nz = lax.axis_size("dp") // 2
     d = activations.shape[1]
-    half, quarter = d // 2, d // 8
+    half = d // 2
+    slots = max(nz // 8, 1)
+    regions, part = nz // slots, slots * LANES
     tok, width = grad_query.shape
     vm = pltpu.VMEM
     side = max(nx, ny)
@@ -352,10 +371,10 @@
         vm((2, d, LANES), BF16),
         vm((tn, 16, LANES), BF16),
         vm((2 * tn * 16, LANES), BF16),
-        vm((4, side, side, RANK, quarter), F32),
-        vm((4, side, side, RANK, quarter), F32),
-        vm((4, side, RANK, quarter), F32),
-        vm((4, side, RANK, quarter), F32),
+        vm((regions, side, side, RANK, part), F32),
+        vm((regions, side, side, RANK, part), F32),
+        vm((regions, side, RANK, part), F32),
+        vm((regions, side, RANK, part), F32),
         vm((2, nz, RANK, LANES), F32),
         vm((nz, RANK, LANES), F32),
         vm((nz, RANK, LANES), F32),
@@ -363,7 +382,6 @@
         vm((nx, ny, nz, 16, LANES), BF16),
         vm((nz, 16, LANES), BF16),
         vm((RANK, d), F32),
-        vm((tn * 16, 2 * LANES), F32),
         vm((tn, RANK, 2 * LANES), F32),
         vm((2 * tn, RANK, 2 * LANES), F32),
         vm((nz, RANK, LANES), F32),
@@ -384,7 +402,7 @@
         out_specs=(anywhere, pl.BlockSpec(memory_space=pltpu.VMEM)),
         scratch_shapes=scratch,
         compiler_params=pltpu.CompilerParams(
-            collective_id=0, has_side_effects=True, vmem_limit_bytes=60 * 1024 * 1024
+            collective_id=0, has_side_effects=True, vmem_limit_bytes=54600 * 1024
         ),
     )(start_factor, grad_query, activations, feedback)
 

time: 79.8 us -> 72.8 us (0.912)
  Pallas kernels: 76 us -> 70 us
  local copies, waits for them, and re-layouts: 2.86 us -> 1.95 us
    pallas_call x1, Pallas kernels: 76 us -> 70 us  [body(): pl.pallas_call(functools.partial(kernel, nx, ny, nz), out_shape=(jax.Shap...]
    unnamed x2 -> x4, local copies, waits for them, and re-layouts: 2.86 us -> 1.95 us
where the time goes in v3:
time: 72.8 us; the launch traced here: 72.6 us
  Pallas kernels  70 us (96%)
  local copies, waits for them, and re-layouts  1.95 us (3%)
    pallas_call x1, Pallas kernels, body(): pl.pallas_call(functools.partial(kernel, nx, ny, nz), out_shape=(jax.Shap...  70 us
    unnamed x4, local copies, waits for them, and re-layouts  1.95 us

profile of v3, /device:TPU:1, one launch (start us, length us, event | category | flops | bytes accessed | tf_op | source)
XLA Modules:
  0.0 72.6 jit_solution(5277057179269991946)
XLA Ops:
  0.6 0.0 copy-start
  0.6 0.7 copy-done
  1.3 70.0 %shard_map.59 = (f32[8,4096]{1,0:T(8,128)S(1)}, f32[8,256]{1,0:T(8,128)S(1)}) custom-call(f32[8,256]{1,0:T(8,128)S(1)} %copy-done, bf16[2048,256]{1,0:T(8,128)(2,1)} %g_hbm.1, bf16[128,4096]{1,0:T(8,128)(2,1)} %a_hbm.1, bf16[4096,256]{1,0:T(8,128)(2,1)} %f_hbm.1), custom_call_target="tpu_custom_call" | custom-call | tf_op jit(solution)/shard_map/pallas_call | solution.py:395
  71.4 0.7 copy.8
  72.0 0.6 copy.9
Async XLA Ops:
  0.6 0.7 copy-start

commit v4 on v3

--- a/solution.py
+++ b/solution.py
@@ -93,7 +93,7 @@
     for dx, dy, dc in itertools.product(range(nx), range(ny), range(2)):
         if dx + dy + dc:
             group = xs[dx] * ny + ys[dy]
-            plane.append((hops(dx, nx) + hops(dy, ny), group, (2 * z + o if dc else dp, group)))
+            plane.append((hops(dx, nx) + hops(dy, ny), group, (2 * z + o if dc else dp, group), not dc))
     plane.sort(key=lambda entry: -entry[0])
     by_distance = sorted(range(1, nz), key=lambda k: -hops(k, nz))
 
@@ -108,7 +108,7 @@
 
     barrier = pltpu.get_barrier_semaphore()
     beside = sorted({1, nz - 1})
-    for _, _, device in plane:
+    for _, _, device, _ in plane:
         pl.semaphore_signal(barrier, inc=1, device_id=device, device_id_type=MESH)
     for k in beside:
         pl.semaphore_signal(barrier, inc=1, device_id=along_z(k), device_id_type=MESH)
@@ -131,7 +131,7 @@
     pl.semaphore_wait(barrier, len(plane) + len(beside))
 
     p_channel = next(counter)
-    for _, group, device in plane:
+    for _, group, device, _ in plane:
         remote(psend.at[group], precv.at[block(c * tn + t, 16), :], p_channel, device).start()
     share_a = remote(a_hbm.at[:, block(o, half)], a_v.at[block(c, LANES), :], next(counter), partner)
     share_a.start()
@@ -264,24 +264,39 @@
         for k in range(1, size):
             remote(line, line, second_channel[r], device(k)).start()
 
+    def columns(slots_of):
+        return jnp.concatenate([features(k) for k in slots_of], axis=1)
+
+    def lines(slots_of):
+        return jnp.concatenate([ball[:, :, k].reshape(tn * 16, LANES) for k in slots_of], axis=1)
+
     def product(r):
         own = part_of(r)
         _, (_, size, _, _) = order(r)
         rest = ball.at[:, pl.ds(0, size - 1), own] if r[1] == 0 else ball.at[pl.ds(0, size - 1), :, own]
         arrived(rest, second_channel[r])
-        left = jnp.concatenate([ball[:, :, k].reshape(tn * 16, LANES) for k in region(r)], axis=1)
-        return dot(left, jnp.concatenate([features(k) for k in region(r)], axis=1), NT)
-
-    for step in range(groups + 2):
-        if step < groups:
-            spread_own((step, 0))
-            spread_own((step, 1))
+        return dot(lines(region(r)), columns(region(r)), NT)
+
+    last = groups - 1
+    opposite = range(start((last, 0)), start((last, 1)) + slots)
+    for step in range(last):
+        spread_own((step, 0))
+        spread_own((step, 1))
         if step >= 2:
             spread_line((step - 2, 0))
             spread_line((step - 2, 1))
-        if step == groups - 1:
-            share_half = remote(ball.at[x, y], other_half, next(counter), partner)
-            share_half.start()
+    for side in range(2):
+        arrived(ball.at[x, y, part_of((last, side))], gather[last, side])
+    straight = next(counter)
+    far = pl.ds(opposite[0], len(opposite))
+    for _, _, device, same in plane:
+        if same:
+            remote(ball.at[x, y, far], ball.at[x, y, far], straight, device).start()
+    share_half = remote(ball.at[x, y], other_half, next(counter), partner)
+    share_half.start()
+    for step in range(max(last - 2, 0), last):
+        spread_line((step, 0))
+        spread_line((step, 1))
 
     share_half.wait()
     pairs = []
@@ -315,11 +330,13 @@
     left = jnp.concatenate([u.astype(BF16) for u in pairs], axis=1)
     right = dot(left, fh_v[0], NN) + dot(left, fh_v[1], NN)
 
-    q2 = sum(product(r) for r in nearest)
+    q2 = sum(product(r) for r in nearest[:-2])
+    arrived(ball.at[pl.ds(0, len(opposite)), 0, pl.ds(0, tn - 1)], straight)
+    q2 = q2 + dot(lines(opposite), columns(opposite), NT)
     for g in range(tn):
         qs[g] = unpair(q2[g * 16:(g + 1) * 16])
     q_channel = next(counter)
-    for _, group, device in plane:
+    for _, group, device, _ in plane:
         remote(qs.at[group], qr.at[c * tn + t], q_channel, device).start()
     qr[c * tn + t] = qs[t]
 

time: 72.8 us -> 71.4 us (0.981)
  Pallas kernels: 70 us -> 68.6 us
    pallas_call x1, Pallas kernels: 70 us -> 68.6 us  [body(): pl.pallas_call(functools.partial(kernel, nx, ny, nz), out_shape=(jax.Shap...]
where the time goes in v4:
time: 71.4 us; the launch traced here: 71.2 us
  Pallas kernels  68.6 us (96%)
  local copies, waits for them, and re-layouts  1.95 us (3%)
    pallas_call x1, Pallas kernels, body(): pl.pallas_call(functools.partial(kernel, nx, ny, nz), out_shape=(jax.Shap...  68.6 us
    unnamed x4, local copies, waits for them, and re-layouts  1.95 us

profile of v4, /device:TPU:1, one launch (start us, length us, event | category | flops | bytes accessed | tf_op | source)
XLA Modules:
  0.0 71.2 jit_solution(5273666871790937355)
XLA Ops:
  0.6 0.0 copy-start
  0.6 0.7 copy-done
  1.3 68.6 %shard_map.59 = (f32[8,4096]{1,0:T(8,128)S(1)}, f32[8,256]{1,0:T(8,128)S(1)}) custom-call(f32[8,256]{1,0:T(8,128)S(1)} %copy-done, bf16[2048,256]{1,0:T(8,128)(2,1)} %g_hbm.1, bf16[128,4096]{1,0:T(8,128)(2,1)} %a_hbm.1, bf16[4096,256]{1,0:T(8,128)(2,1)} %f_hbm.1), custom_call_target="tpu_custom_call" | custom-call | tf_op jit(solution)/shard_map/pallas_call | solution.py:412
  70.0 0.7 copy.8
  70.6 0.6 copy.9
Async XLA Ops:
  0.6 0.7 copy-start

commit v5 on v4

--- a/solution.py
+++ b/solution.py
@@ -103,16 +103,13 @@
     load_f = pltpu.make_async_copy(f_hbm, f_v, local.at[3])
     load_gh = pltpu.make_async_copy(g_hbm.at[:, block(c, LANES)], gh_v.at[c], local.at[4])
     load_fh = pltpu.make_async_copy(f_hbm.at[:, block(c, LANES)], fh_v.at[c], local.at[5])
-    load_s.start()
-    load_g.start()
-
     barrier = pltpu.get_barrier_semaphore()
     beside = sorted({1, nz - 1})
     for _, _, device, _ in plane:
         pl.semaphore_signal(barrier, inc=1, device_id=device, device_id_type=MESH)
     for k in beside:
         pl.semaphore_signal(barrier, inc=1, device_id=along_z(k), device_id_type=MESH)
-    for load in (load_a, load_f, load_gh, load_fh):
+    for load in (load_s, load_g, load_a, load_f, load_gh, load_fh):
         load.start()
 
     reach = [2 ** k for k in range(8) if 2 ** k < nz // 2]
@@ -158,17 +155,23 @@
     def part_of(r):
         return pl.ds(start(r), slots)
 
+    wide = first.shape[-1] // LANES
+
+    def wide_region(r):
+        begin = r[0] * wide if r[1] == 0 else nz - (r[0] + 1) * wide
+        return range(begin, begin + wide)
+
     def index(r):
         return 2 * r[0] + r[1]
 
     nearest = [(i, side) for i in range(groups) for side in range(2)]
-    farthest = [(i, side) for i in reversed(range(groups)) for side in range(2)]
+    farthest = [(i, side) for i in reversed(range(nz // (2 * wide))) for side in range(2)]
 
     lhs = jnp.concatenate([precv[:tn * 16, :], precv[tn * 16:, :]], axis=1)
     first_channel, second_channel = {}, {}
     for r in farthest:
         (here, count, _, device), _ = order(r)
-        part = dot(lhs, jnp.concatenate([features(k) for k in region(r)], axis=1), NN)
+        part = dot(lhs, jnp.concatenate([features(k) for k in wide_region(r)], axis=1), NN)
         for gx in range(nx):
             for gy in range(ny):
                 g = gx * ny + gy
@@ -209,9 +212,9 @@
         total = second[index(r), place]
         for k in range(1, size):
             total = total + second_in[index(r), beyond[k]]
-        for i, k in enumerate(region(r)):
+        for i, k in enumerate(wide_region(r)):
             zs[k] = total[:, i * LANES:(i + 1) * LANES] + (lf[c, around[k]] + lfr[around[k]])
-        for k in sorted(region(r), key=lambda k: -hops(k, nz)):
+        for k in sorted(wide_region(r), key=lambda k: -hops(k, nz)):
             if k:
                 remote(zs.at[k], zr.at[k], z_channel, along_z(k)).start()
 
@@ -282,9 +285,6 @@
     for step in range(last):
         spread_own((step, 0))
         spread_own((step, 1))
-        if step >= 2:
-            spread_line((step - 2, 0))
-            spread_line((step - 2, 1))
     for side in range(2):
         arrived(ball.at[x, y, part_of((last, side))], gather[last, side])
     straight = next(counter)
@@ -294,7 +294,7 @@
             remote(ball.at[x, y, far], ball.at[x, y, far], straight, device).start()
     share_half = remote(ball.at[x, y], other_half, next(counter), partner)
     share_half.start()
-    for step in range(max(last - 2, 0), last):
+    for step in range(last):
         spread_line((step, 0))
         spread_line((step, 1))
 
@@ -353,7 +353,10 @@
     c_channel = next(counter)
     for k in by_distance:
         remote(cr.at[z], cr.at[z], c_channel, along_z(k)).start()
-    arrived(cr.at[pl.ds(0, nz - 1)], c_channel)
+    store_basis.wait()
+    for ref, channel in sent:
+        wait_bytes(ref, send.at[channel])
+    wait_bytes(cr.at[pl.ds(0, nz - 1)], recv.at[c_channel])
     total = cr[0]
     for k in range(1, nz):
         total = total + cr[k]
@@ -363,9 +366,7 @@
     share_c = remote(cfin, coeffs_ref.at[:, block(c, LANES)], next(counter), partner)
     share_c.start()
 
-    store_basis.wait()
-    for ref, channel in sent:
-        wait_bytes(ref, send.at[channel])
+    wait_bytes(cr.at[pl.ds(0, nz - 1)], send.at[c_channel])
     share_c.wait()
 
 
@@ -374,8 +375,8 @@
     nz = lax.axis_size("dp") // 2
     d = activations.shape[1]
     half = d // 2
-    slots = max(nz // 8, 1)
-    regions, part = nz // slots, slots * LANES
+    wide = max(nz // 4, 1)
+    regions, part = nz // wide, wide * LANES
     tok, width = grad_query.shape
     vm = pltpu.VMEM
     side = max(nx, ny)

time: 71.4 us -> 70.9 us (level)
  no operation moved by 1% of the time
where the time goes in v5:
time: 70.9 us; the launch traced here: 70.8 us
  Pallas kernels  68.2 us (96%)
  local copies, waits for them, and re-layouts  1.95 us (3%)
    pallas_call x1, Pallas kernels, body(): pl.pallas_call(functools.partial(kernel, nx, ny, nz), out_shape=(jax.Shap...  68.2 us
    unnamed x4, local copies, waits for them, and re-layouts  1.95 us

profile of v5, /device:TPU:1, one launch (start us, length us, event | category | flops | bytes accessed | tf_op | source)
XLA Modules:
  0.0 70.8 jit_solution(17355242767718237911)
XLA Ops:
  0.6 0.0 copy-start
  0.6 0.7 copy-done
  1.3 68.2 %shard_map.59 = (f32[8,4096]{1,0:T(8,128)S(1)}, f32[8,256]{1,0:T(8,128)S(1)}) custom-call(f32[8,256]{1,0:T(8,128)S(1)} %copy-done, bf16[2048,256]{1,0:T(8,128)(2,1)} %g_hbm.1, bf16[128,4096]{1,0:T(8,128)(2,1)} %a_hbm.1, bf16[4096,256]{1,0:T(8,128)(2,1)} %f_hbm.1), custom_call_target="tpu_custom_call" | custom-call | tf_op jit(solution)/shard_map/pallas_call | solution.py:413
  69.5 0.7 copy.8
  70.2 0.6 copy.9
Async XLA Ops:
  0.6 0.7 copy-start

commit v6 on v5

--- a/solution.py
+++ b/solution.py
@@ -258,14 +258,19 @@
         for k in range(1, count):
             remote(ball.at[x, y, own], ball.at[x, y, own], first_channel[r], device(k)).start()
 
-    def spread_line(r):
-        own = part_of(r)
-        (_, count, _, _), (_, size, _, device) = order(r)
-        arrived(ball.at[x, pl.ds(0, count - 1), own], first_channel[r])
-        second_channel[r] = next(counter)
-        line = ball.at[:, y, own] if r[1] == 0 else ball.at[x, :, own]
+    def span(members, side):
+        begin = start((members[-1] if side else members[0], side))
+        return range(begin, begin + len(members) * slots)
+
+    def spread_lines(members, side):
+        (_, count, _, _), (_, size, _, device) = order((0, side))
+        for i in members:
+            arrived(ball.at[x, pl.ds(0, count - 1), part_of((i, side))], first_channel[i, side])
+        own = pl.ds(span(members, side)[0], len(members) * slots)
+        second_channel[members[0], side] = next(counter)
+        line = ball.at[x, :, own] if side else ball.at[:, y, own]
         for k in range(1, size):
-            remote(line, line, second_channel[r], device(k)).start()
+            remote(line, line, second_channel[members[0], side], device(k)).start()
 
     def columns(slots_of):
         return jnp.concatenate([features(k) for k in slots_of], axis=1)
@@ -273,12 +278,13 @@
     def lines(slots_of):
         return jnp.concatenate([ball[:, :, k].reshape(tn * 16, LANES) for k in slots_of], axis=1)
 
-    def product(r):
-        own = part_of(r)
-        _, (_, size, _, _) = order(r)
-        rest = ball.at[:, pl.ds(0, size - 1), own] if r[1] == 0 else ball.at[pl.ds(0, size - 1), :, own]
-        arrived(rest, second_channel[r])
-        return dot(lines(region(r)), columns(region(r)), NT)
+    def product(members, side):
+        chunks = span(members, side)
+        own = pl.ds(chunks[0], len(chunks))
+        size = order((0, side))[1][1]
+        rest = ball.at[pl.ds(0, size - 1), :, own] if side else ball.at[:, pl.ds(0, size - 1), own]
+        arrived(rest, second_channel[members[0], side])
+        return dot(lines(chunks), columns(chunks), NT)
 
     last = groups - 1
     opposite = range(start((last, 0)), start((last, 1)) + slots)
@@ -294,9 +300,10 @@
             remote(ball.at[x, y, far], ball.at[x, y, far], straight, device).start()
     share_half = remote(ball.at[x, y], other_half, next(counter), partner)
     share_half.start()
-    for step in range(last):
-        spread_line((step, 0))
-        spread_line((step, 1))
+    joined = [list(range(last - 1)), [last - 1]] if last > 1 else [[0]]
+    for members in joined:
+        for side in range(2):
+            spread_lines(members, side)
 
     share_half.wait()
     pairs = []
@@ -330,7 +337,7 @@
     left = jnp.concatenate([u.astype(BF16) for u in pairs], axis=1)
     right = dot(left, fh_v[0], NN) + dot(left, fh_v[1], NN)
 
-    q2 = sum(product(r) for r in nearest[:-2])
+    q2 = sum(product(members, side) for members in joined for side in range(2))
     arrived(ball.at[pl.ds(0, len(opposite)), 0, pl.ds(0, tn - 1)], straight)
     q2 = q2 + dot(lines(opposite), columns(opposite), NT)
     for g in range(tn):

time: 70.9 us -> 71.4 us (level)
  no operation moved by 1% of the time
where the time goes in v6:
time: 71.4 us; the launch traced here: 71.3 us
  Pallas kernels  68.7 us (96%)
  local copies, waits for them, and re-layouts  1.95 us (3%)
    pallas_call x1, Pallas kernels, body(): pl.pallas_call(functools.partial(kernel, nx, ny, nz), out_shape=(jax.Shap...  68.7 us
    unnamed x4, local copies, waits for them, and re-layouts  1.95 us

profile of v6, /device:TPU:1, one launch (start us, length us, event | category | flops | bytes accessed | tf_op | source)
XLA Modules:
  0.0 71.3 jit_solution(10873366399901169353)
XLA Ops:
  0.6 0.0 copy-start
  0.6 0.7 copy-done
  1.3 68.7 %shard_map.59 = (f32[8,4096]{1,0:T(8,128)S(1)}, f32[8,256]{1,0:T(8,128)S(1)}) custom-call(f32[8,256]{1,0:T(8,128)S(1)} %copy-done, bf16[2048,256]{1,0:T(8,128)(2,1)} %g_hbm.1, bf16[128,4096]{1,0:T(8,128)(2,1)} %a_hbm.1, bf16[4096,256]{1,0:T(8,128)(2,1)} %f_hbm.1), custom_call_target="tpu_custom_call" | custom-call | tf_op jit(solution)/shard_map/pallas_call | solution.py:420
  70.0 0.7 copy.8
  70.7 0.6 copy.9
Async XLA Ops:
  0.6 0.7 copy-start
